TPU v7x, 32 devices: a whole 2x2x4 slice. The times are simulated.
32 devices in a mesh: dp: 4 (over y, x), group: 8 (over z, core).
Axes of the slice: x: 2, y: 2, z: 4, core: 2. Of those that a mesh axis runs over, the one named last changes fastest.
Arguments:
- partials: bfloat16 [4, 4, 7168, 2048], P('dp', None, 'group'), may hold values from -25 to 25
- momentum: float32 [4, 7168, 2048], P('dp', 'group'), may hold values from -6 to 6
Outputs:
- momentum_out: float32 [4, 7168, 2048], P('dp', 'group')
- update: bfloat16 [4, 7168, 2048], P('dp', 'group')
All inputs are finite; a program needn't handle non-finite values.
Results may differ from a plain program's by a relative error of at most 0.034.
Values may be sent and summed in bfloat16 or wider, within the bound.
A program may use at most 128 MiB of HBM per device.

v0:
```python
import math

import jax
import jax.numpy as jnp
from jax import lax
from jax.sharding import PartitionSpec as P

C = 7168


def orthogonal(block):
    rows_total = block.shape[1]
    gram_slab = lax.psum_scatter(
        lax.dot_general(
            block, block, (((0,), (0,)), ((), ())), preferred_element_type=jnp.float32
        ).astype(jnp.bfloat16),
        "group",
        scatter_dimension=0,
        tiled=True,
    )
    wide = block.astype(jnp.float32)
    total = lax.psum(jnp.sum(wide * wide), "group")
    gram_full = lax.all_gather(gram_slab, "group", axis=0, tiled=True)
    scale2 = 2.0 * (total + 1e-06) / rows_total
    first = (
        lax.dot_general(
            block, gram_full, (((1,), (1,)), ((), ())), preferred_element_type=jnp.float32
        )
        / scale2
    ).astype(jnp.bfloat16)
    second = (
        lax.dot_general(
            first, gram_full, (((1,), (1,)), ((), ())), preferred_element_type=jnp.float32
        )
        / scale2
    )
    ortho = (
        3.4445 * block.astype(jnp.float32) - 4.775 * first.astype(jnp.float32) + 2.0315 * second
    ) / jnp.sqrt(scale2)
    return (ortho * math.sqrt(C)).astype(jnp.bfloat16)


def shards(partials, momentum):
    grad = lax.psum_scatter(partials[0], "dp", scatter_dimension=0, tiled=True).astype(jnp.float32)
    momentum_out = 0.95 * momentum + grad
    blended = (grad + 0.95 * momentum_out).astype(jnp.bfloat16)
    results = [orthogonal(blended[0])]
    return (momentum_out, jnp.stack(results))


def solution(mesh):
    return jax.shard_map(
        shards,
        mesh=mesh,
        in_specs=(P("dp", None, "group", None), P("dp", "group", None)),
        out_specs=(P("dp", "group", None), P("dp", "group", None)),
        check_vma=False,
    )
```

profile of v0, /device:TPU:1, one launch (start us, length us, event | category | flops | bytes accessed | tf_op | source)
XLA Modules:
  0.0 377.3 jit_solution(13129221017275234228)
XLA Ops:
  7.2 0.0 reduce-scatter.7.cloned.1.call-start
  7.2 0.7 reduce-scatter.7.cloned.1.call-update
  7.9 0.0 reduce-scatter.5.cloned.1.call-start
  7.9 143.2 %reduce-scatter.7.cloned.1.call-done = bf16[1,896,2048]{2,1,0:T(8,128)(2,1)} async-done(((bf16[4,896,2048]{2,1,0:T(8,128)(2,1)}), bf16[1,896,2048]{2,1,0:T(8,128)(2,1)}) %reduce-scatter.7.cloned.1.call-update) | async-done | bytes 3670032
  151.1 7.8 %fusion.5 = (f32[]{:T(128)}, bf16[896,2048]{1,0:T(8,128)(2,1)S(1)}, f32[1,896,2048]{2,1,0:T(8,128)}) fusion(bf16[1,896,2048]{2,1,0:T(8,128)(2,1)} %reduce-scatter.7.cloned.1.call-done, f32[1,896,2048]{2,1,0:T(8,128)} %param.3), kind=kLoop, calls=%fused_computation.10 | loop fusion | flops 16515071 | bytes 22020100 | tf_op jit(solution)/shard_map/reduce_sum | solution.py:22
  158.9 0.0 copy-start
  158.9 1.8 copy-done
  160.7 11.4 %convolution_convert_fusion = bf16[2048,2048]{1,0:T(8,128)(2,1)} fusion(bf16[896,2048]{1,0:T(8,128)(2,1)S(1)} %get-tuple-element.3), kind=kOutput, calls=%fused_computation.4 | convolution fusion | flops 7520387072 | bytes 12058624 | tf_op jit(solution)/shard_map/dot_general | solution.py:14
  172.1 0.0 reduce-scatter.5.cloned.1.call-update
  172.1 0.0 all-gather.2.cloned.1.call-start
  172.2 87.6 %reduce-scatter.5.cloned.1.call-done = bf16[256,2048]{1,0:T(8,128)(2,1)} async-done(((bf16[2048,2048]{1,0:T(8,128)(2,1)}), bf16[256,2048]{1,0:T(8,128)(2,1)}) %reduce-scatter.5.cloned.1.call-update) | async-done | bytes 1048592 | tf_op jit(solution)/shard_map/reduce_scatter | solution.py:13
  259.7 0.0 all-gather.2.cloned.1.call-update
  259.8 16.6 %psum.7 = f32[]{:T(128)} all-reduce(f32[]{:T(128)} %get-tuple-element.2), channel_id=1, replica_groups=mesh['dp'=4,'group'=8] {'group'}, use_global_device_ids=true, to_apply=%region_3.0 | all-reduce | flops 1 | bytes 8 | tf_op jit(solution)/shard_map/psum | solution.py:22
  277.1 67.3 %all-gather.2.cloned.1.call-done = bf16[2048,2048]{1,0:T(8,128)(2,1)} async-done(((bf16[256,2048]{1,0:T(8,128)(2,1)}), bf16[2048,2048]{1,0:T(8,128)(2,1)}) %all-gather.2.cloned.1.call-update) | async-done | bytes 8388624 | tf_op jit(solution)/shard_map/all_gather | solution.py:23
  344.4 0.0 copy-start.1
  344.4 0.0 copy-start.2
  344.4 13.3 %divide_convert_fusion = bf16[896,2048]{1,0:T(8,128)(2,1)} fusion(bf16[896,2048]{1,0:T(8,128)(2,1)} %copy-done, bf16[2048,2048]{1,0:T(8,128)(2,1)} %all-gather.2.cloned.1.call-done, f32[]{:T(128)S(6)} %div.19), kind=kOutput, calls=%fused_computation.11 | convolution fusion | flops 7519862784 | bytes 15728644 | tf_op jit(solution)/shard_map/dot_general | solution.py:26
  357.7 0.0 copy-done.1
  357.7 0.0 copy-done.2
  357.7 13.1 %fusion.8 = bf16[1,896,2048]{2,1,0:T(8,128)(2,1)} fusion(f32[]{:T(128)S(6)} %sqrt.3, f32[]{:T(128)S(6)} %div.19, bf16[896,2048]{1,0:T(8,128)(2,1)} %divide_convert_fusion, bf16[2048,2048]{1,0:T(8,128)(2,1)S(1)} %copy-done.2, bf16[896,2048]{1,0:T(8,128)(2,1)S(1)} %copy-done.1), kind=kOutput, calls=%fused_computation.14 | convolution fusion | flops 7536377856 | bytes 19398664 | tf_op jit(solution)/shard_map/dot_general | solution.py:32
Async XLA Ops:
  7.2 144.0 %reduce-scatter.7.cloned.1.call-start = ((), (), s32[]{:S(2)}) async-start(), calls=%async_computation.4 | async-start | bytes 18350080
  7.9 251.8 %reduce-scatter.5.cloned.1.call-start = ((), (), s32[]{:S(2)}) async-start(), calls=%async_computation.2 | async-start | bytes 9437184 | tf_op jit(solution)/shard_map/reduce_scatter | solution.py:13
  158.9 1.8 copy-start
  172.1 172.2 %all-gather.2.cloned.1.call-start = ((), (), s32[]{:S(2)}) async-start(), calls=%async_computation.3 | async-start | bytes 9437184 | tf_op jit(solution)/shard_map/all_gather | solution.py:23
  344.4 13.3 %copy-start.1 = (bf16[896,2048]{1,0:T(8,128)(2,1)S(1)}, bf16[896,2048]{1,0:T(8,128)(2,1)}, u32[]{:S(2)}) copy-start(bf16[896,2048]{1,0:T(8,128)(2,1)} %copy-done) | copy-start | bytes 11010052
  344.4 13.3 %copy-start.2 = (bf16[2048,2048]{1,0:T(8,128)(2,1)S(1)}, bf16[2048,2048]{1,0:T(8,128)(2,1)}, u32[]{:S(2)}) copy-start(bf16[2048,2048]{1,0:T(8,128)(2,1)} %all-gather.2.cloned.1.call-done) | copy-start | bytes 25165828
Sparse Core Ops, SparseCore 0:
  11.1 139.9 reduce-scatter.6
  172.2 87.4 reduce-scatter.4
  261.3 82.9 all-gather.1
where the time goes:
time: 378 us; the launch traced here: 377 us
  waiting for transfers between devices  299 us (79%)
  matrix products  37.8 us (10%)
  blocking collectives  16.6 us (4%)
  between operations  14.5 us (4%)
  other arithmetic  7.75 us (2%)
    unnamed x4, waiting for transfers between devices  144 us
    reduce_scatter x1, waiting for transfers between devices, orthogonal(): lax.psum_scatter(lax.dot_general(block, block, (((0,), (0,)), ((), ())),...  87.6 us
    all_gather x1, waiting for transfers between devices, orthogonal(): gram_full = lax.all_gather(gram_slab, 'group', axis=0, tiled=True)  67.3 us
    psum x1, blocking collectives, orthogonal(): total = lax.psum(jnp.sum(wide * wide), 'group')  16.6 us
    dot_general x1, matrix products, orthogonal(): lax.dot_general(block, gram_full, (((1,), (1,)), ((), ())), preferred_ele...  13.3 us
    dot_general x1, matrix products, orthogonal(): lax.dot_general(first, gram_full, (((1,), (1,)), ((), ())), preferred_ele...  13.1 us
    dot_general x1, matrix products, orthogonal(): lax.dot_general(block, block, (((0,), (0,)), ((), ())), preferred_element...  11.4 us
    reduce_sum x1, other arithmetic, orthogonal(): total = lax.psum(jnp.sum(wide * wide), 'group')  7.75 us
  transfers between devices with their start and end apart: 3, of which 3 were waited for; matrix products, arithmetic and copies ran while one was open for 0% of the time, Pallas kernels for 0%

commit v1 on v0

--- a/solution.py
+++ b/solution.py
@@ -1,11 +1,17 @@
+import functools
 import math
 
 import jax
 import jax.numpy as jnp
 from jax import lax
+from jax.experimental import pallas as pl
+from jax.experimental.pallas import tpu as pltpu
 from jax.sharding import PartitionSpec as P
 
 C = 7168
+NB = 8
+WINDOW = 2
+MESH = pl.DeviceIdType.MESH
 
 
 def orthogonal(block):
@@ -48,9 +54,447 @@
     return (momentum_out, jnp.stack(results))
 
 
+def sum_kernel(
+    partials,
+    momentum,
+    mom_hbm,
+    x_hbm,
+    gram_hbm,
+    via,
+    near,
+    far,
+    relay_own,
+    x,
+    mom,
+    xt,
+    gram,
+    part,
+    pair_out,
+    pair_in,
+    chain,
+    sums,
+    load_sem,
+    dp_send,
+    dp_recv,
+    pair_send,
+    pair_recv,
+    red_send,
+    red_recv,
+    bc_send,
+    bc_recv,
+    sib_send,
+    sib_recv,
+    store_sem,
+):
+    rows, cols = x.shape
+    blk = cols // NB
+    half = rows // 2
+    dp = lax.axis_index("dp")
+    group = lax.axis_index("group")
+    y, xx = dp // 2, dp % 2
+    z, core = group // 2, group % 2
+    at_x, at_y, at_diag = y * 2 + (1 - xx), (1 - y) * 2 + xx, (1 - y) * 2 + (1 - xx)
+    other = 1 - core
+    sibling = (dp, z * 2 + other)
+
+    barrier = pltpu.get_barrier_semaphore()
+    for peer in (
+        (at_x, group),
+        (at_y, group),
+        sibling,
+        (dp, lax.rem(z + 1, 4) * 2 + core),
+        (dp, lax.rem(z + 3, 4) * 2 + core),
+    ):
+        pl.semaphore_signal(barrier, inc=1, device_id=peer, device_id_type=MESH)
+    pl.semaphore_wait(barrier, 5)
+
+    span = [slice(0, half), slice(half, rows)]
+    hop1 = [at_x, at_y]
+    hop2 = [at_y, at_x]
+
+    def col(k):
+        return slice(k * blk, (k + 1) * blk)
+
+    def dp_copy(kind, p, k):
+        src, dst, to = (
+            (partials.at[0, at_diag, span[p], col(k)], via, hop1[p]),
+            (partials.at[0, hop1[p], span[p], col(k)], near, hop1[p]),
+            (via.at[span[p], col(k)], far, hop2[p]),
+        )[kind]
+        return pltpu.make_async_remote_copy(
+            src_ref=src,
+            dst_ref=dst.at[span[p], col(k)],
+            send_sem=dp_send.at[kind, p, k],
+            recv_sem=dp_recv.at[kind, p, k],
+            device_id=(to, group),
+            device_id_type=MESH,
+        )
+
+    def loads(k):
+        copies = [
+            pltpu.make_async_copy(
+                partials.at[0, hop2[p], span[p], col(k)],
+                relay_own.at[span[p], col(k)],
+                load_sem.at[p, k],
+            )
+            for p in range(2)
+        ]
+        copies.append(
+            pltpu.make_async_copy(
+                partials.at[0, dp, :, col(k)], x.at[:, col(k)], load_sem.at[2, k]
+            )
+        )
+        copies.append(
+            pltpu.make_async_copy(
+                momentum.at[0, :, col(k)], mom.at[:, col(k)], load_sem.at[3, k]
+            )
+        )
+        return copies
+
+    def stores(k):
+        top = (k + 1) * blk
+        return [
+            pltpu.make_async_copy(mom.at[:, col(k)], mom_hbm.at[:, col(k)], store_sem.at[0, k]),
+            pltpu.make_async_copy(x.at[:, col(k)], x_hbm.at[:, col(k)], store_sem.at[1, k]),
+            pltpu.make_async_copy(
+                gram.at[0:top, col(k)], gram_hbm.at[0:top, col(k)], store_sem.at[2, k]
+            ),
+        ]
+
+    def send_first(k):
+        for kind in (0, 1):
+            for p in range(2):
+                dp_copy(kind, p, k).start()
+
+    def forward(k):
+        for p in range(2):
+            dp_copy(0, p, k).wait_recv()
+            loads(k)[p].wait()
+            at = (span[p], col(k))
+            via[at] = (
+                via[at].astype(jnp.float32) + relay_own[at].astype(jnp.float32)
+            ).astype(jnp.bfloat16)
+            dp_copy(2, p, k).start()
+
+    def unit(k):
+        return (k + 1) * blk // 4
+
+    def packed(k, h=None):
+        start = blk // 4 * k * (k + 1)
+        if h is None:
+            return slice(start, start + 2 * unit(k))
+        return slice(start + h * unit(k), start + (h + 1) * unit(k))
+
+    def pair_copy(k):
+        return pltpu.make_async_remote_copy(
+            src_ref=pair_out.at[packed(k)],
+            dst_ref=pair_in.at[packed(k)],
+            send_sem=pair_send.at[k],
+            recv_sem=pair_recv.at[k],
+            device_id=sibling,
+            device_id_type=MESH,
+        )
+
+    def blend(k):
+        for copy in loads(k)[2:]:
+            copy.wait()
+        for kind in (1, 2):
+            for p in range(2):
+                dp_copy(kind, p, k).wait_recv()
+        at = (slice(None), col(k))
+        grad = (
+            x[at].astype(jnp.float32) + near[at].astype(jnp.float32) + far[at].astype(jnp.float32)
+        )
+        state = 0.95 * mom[at] + grad
+        mom[at] = state
+        mixed = grad + 0.95 * state
+        x[at] = mixed.astype(jnp.bfloat16)
+        xt[col(k), :] = mixed.T.astype(jnp.bfloat16)
+        for copy in stores(k)[:2]:
+            copy.start()
+        own = x[at]
+
+        @pl.loop(0, k + 1)
+        def _(r):
+            strip = pl.ds(pl.multiple_of(r * blk, blk), blk)
+            part[strip, :] = jnp.dot(xt[strip, :], own, preferred_element_type=jnp.float32)
+
+        n = 2 * unit(k)
+        pair_out[packed(k), :] = part[pl.ds(pl.multiple_of(other * n, n), n), :].astype(
+            jnp.bfloat16
+        )
+        pair_copy(k).start()
+
+    place = [z, 3 - z]
+
+    def chip_at(h, spot):
+        return spot if h == 0 else 3 - spot
+
+    def final(k, h, owner):
+        n = unit(k)
+        return gram.at[pl.ds(pl.multiple_of(owner * 2 * n + h * n, n), n), col(k)]
+
+    def red_copy(k, h, to_spot, slot):
+        return pltpu.make_async_remote_copy(
+            src_ref=sums.at[packed(k, h)],
+            dst_ref=chain.at[slot, packed(k, h)],
+            send_sem=red_send.at[h, k],
+            recv_sem=red_recv.at[slot, h, k],
+            device_id=(dp, chip_at(h, to_spot) * 2 + core),
+            device_id_type=MESH,
+        )
+
+    def bc_copy(k, h, to_spot, slot):
+        return pltpu.make_async_remote_copy(
+            src_ref=final(k, h, core),
+            dst_ref=final(k, h, core),
+            send_sem=bc_send.at[slot, h, k],
+            recv_sem=bc_recv.at[h, k],
+            device_id=(dp, chip_at(h, to_spot) * 2 + core),
+            device_id_type=MESH,
+        )
+
+    def sib_copy(k, h):
+        return pltpu.make_async_remote_copy(
+            src_ref=final(k, h, core),
+            dst_ref=final(k, h, core),
+            send_sem=sib_send.at[h, k],
+            recv_sem=sib_recv.at[h, k],
+            device_id=sibling,
+            device_id_type=MESH,
+        )
+
+    def pair_sum(k):
+        pair_copy(k).wait_recv()
+        n = 2 * unit(k)
+        sums[packed(k), :] = (
+            part[pl.ds(pl.multiple_of(core * n, n), n), :]
+            + pair_in[packed(k), :].astype(jnp.float32)
+        ).astype(jnp.bfloat16)
+        for h in range(2):
+
+            @pl.when(place[h] == 0)
+            def _():
+                red_copy(k, h, 1, 0).start()
+
+            @pl.when(place[h] == 3)
+            def _():
+                red_copy(k, h, 2, 0).start()
+
+    def relay(k):
+        for h in range(2):
+
+            @pl.when(place[h] == 2)
+            def _():
+                at = packed(k, h)
+                red_copy(k, h, 2, 0).wait_recv()
+                sums[at, :] = (
+                    sums[at, :].astype(jnp.float32) + chain[0, at, :].astype(jnp.float32)
+                ).astype(jnp.bfloat16)
+                red_copy(k, h, 1, 1).start()
+
+    def root(k):
+        for h in range(2):
+
+            @pl.when(place[h] == 1)
+            def _():
+                at = packed(k, h)
+                red_copy(k, h, 1, 0).wait_recv()
+                red_copy(k, h, 1, 1).wait_recv()
+                final(k, h, core)[...] = (
+                    sums[at, :].astype(jnp.float32)
+                    + chain[0, at, :].astype(jnp.float32)
+                    + chain[1, at, :].astype(jnp.float32)
+                ).astype(jnp.bfloat16)
+                bc_copy(k, h, 2, 1).start()
+                bc_copy(k, h, 0, 0).start()
+                sib_copy(k, h).start()
+
+    def spread(k):
+        for h in range(2):
+
+            @pl.when(place[h] == 2)
+            def _():
+                bc_copy(k, h, 2, 1).wait_recv()
+                bc_copy(k, h, 3, 0).start()
+                sib_copy(k, h).start()
+
+    def leaf(k):
+        for h in range(2):
+
+            @pl.when((place[h] == 0) | (place[h] == 3))
+            def _():
+                bc_copy(k, h, 0, 0).wait_recv()
+                sib_copy(k, h).start()
+
+    def finish(k):
+        for h in range(2):
+            sib_copy(k, h).wait_recv()
+        stores(k)[2].start()
+
+    for k in range(WINDOW):
+        send_first(k)
+    for k in range(NB):
+        for copy in loads(k):
+            copy.start()
+
+    stages = (
+        (0, forward),
+        (0, lambda k: send_first(k + WINDOW) if k + WINDOW < NB else None),
+        (4, spread),
+        (5, leaf),
+        (6, finish),
+        (2, blend),
+        (3, relay),
+        (2, pair_sum),
+        (3, root),
+    )
+    for step in range(NB + 6):
+        for lag, stage in stages:
+            if 0 <= step - lag < NB:
+                stage(step - lag)
+
+    for k in range(NB):
+        for copy in stores(k):
+            copy.wait()
+        for p in range(2):
+            for kind in range(3):
+                dp_copy(kind, p, k).wait_send()
+        pair_copy(k).wait_send()
+        for h in range(2):
+            sib_copy(k, h).wait_send()
+
+            @pl.when(place[h] != 1)
+            def _():
+                red_copy(k, h, 1, 0).wait_send()
+
+            @pl.when((place[h] == 1) | (place[h] == 2))
+            def _():
+                bc_copy(k, h, 0, 0).wait_send()
+
+            @pl.when(place[h] == 1)
+            def _():
+                bc_copy(k, h, 2, 1).wait_send()
+
+
+def finish_kernel(x_ref, gram_ref, mom_ref, mom_out, update, first):
+    cols = x_ref.shape[1]
+    blk = cols // NB
+    mom_out[...] = mom_ref[...]
+    eye = lax.broadcasted_iota(jnp.int32, (blk, blk), 0) == lax.broadcasted_iota(
+        jnp.int32, (blk, blk), 1
+    )
+    trace = jnp.zeros((blk, blk), jnp.float32)
+    for k in range(NB):
+        at = slice(k * blk, (k + 1) * blk)
+        trace += jnp.where(eye, gram_ref[at, at].astype(jnp.float32), 0.0)
+    total = jnp.sum(trace) + 1e-06
+    scale2 = jnp.full((1, blk), 2.0 / cols, jnp.float32) * total
+    inv = 1.0 / scale2
+    last = lax.rsqrt(scale2) * math.sqrt(C)
+
+    def times_gram(left, k):
+        at, split = slice(k * blk, (k + 1) * blk), (k + 1) * blk
+        acc = jnp.dot(
+            left[:, :split], gram_ref[:split, at], preferred_element_type=jnp.float32
+        )
+        if split < cols:
+            acc += lax.dot_general(
+                left[:, split:],
+                gram_ref[at, split:],
+                (((1,), (1,)), ((), ())),
+                preferred_element_type=jnp.float32,
+            )
+        return acc
+
+    for k in range(NB):
+        first[:, k * blk : (k + 1) * blk] = (times_gram(x_ref, k) * inv).astype(jnp.bfloat16)
+    for k in range(NB):
+        at = slice(k * blk, (k + 1) * blk)
+        second = times_gram(first, k) * inv
+        ortho = (
+            3.4445 * x_ref[:, at].astype(jnp.float32)
+            - 4.775 * first[:, at].astype(jnp.float32)
+            + 2.0315 * second
+        )
+        update[:, at] = (ortho * last).astype(jnp.bfloat16)
+
+
+def kernels(partials, momentum):
+    _, _, rows, cols = partials.shape
+    blk = cols // NB
+    packed_rows = blk // 4 * NB * (NB + 1)
+    bf16, f32 = jnp.bfloat16, jnp.float32
+    dma = pltpu.SemaphoreType.DMA
+    mom_new, x, gram = pl.pallas_call(
+        sum_kernel,
+        out_shape=(
+            jax.ShapeDtypeStruct((rows, cols), f32),
+            jax.ShapeDtypeStruct((rows, cols), bf16),
+            jax.ShapeDtypeStruct((cols, cols), bf16),
+        ),
+        in_specs=[pl.BlockSpec(memory_space=pl.ANY)] * 2,
+        out_specs=[pl.BlockSpec(memory_space=pl.ANY)] * 3,
+        scratch_shapes=[
+            pltpu.VMEM((rows, cols), bf16),
+            pltpu.VMEM((rows, cols), bf16),
+            pltpu.VMEM((rows, cols), bf16),
+            pltpu.VMEM((rows, cols), bf16),
+            pltpu.VMEM((rows, cols), bf16),
+            pltpu.VMEM((rows, cols), f32),
+            pltpu.VMEM((cols, rows), bf16),
+            pltpu.VMEM((cols, cols), bf16),
+            pltpu.VMEM((cols, blk), f32),
+            pltpu.VMEM((packed_rows, blk), bf16),
+            pltpu.VMEM((packed_rows, blk), bf16),
+            pltpu.VMEM((2, packed_rows, blk), bf16),
+            pltpu.VMEM((packed_rows, blk), bf16),
+            dma((4, NB)),
+            dma((3, 2, NB)),
+            dma((3, 2, NB)),
+            dma((NB,)),
+            dma((NB,)),
+            dma((2, NB)),
+            dma((2, 2, NB)),
+            dma((2, 2, NB)),
+            dma((2, NB)),
+            dma((2, NB)),
+            dma((2, NB)),
+            dma((3, NB)),
+        ],
+        compiler_params=pltpu.CompilerParams(
+            collective_id=0, has_side_effects=True, vmem_limit_bytes=60 * 2**20
+        ),
+        name="sum_and_gram",
+    )(partials, momentum)
+    tile = rows // 2
+    momentum_out, update = pl.pallas_call(
+        finish_kernel,
+        grid=(rows // tile,),
+        out_shape=(
+            jax.ShapeDtypeStruct((rows, cols), f32),
+            jax.ShapeDtypeStruct((rows, cols), bf16),
+        ),
+        in_specs=[
+            pl.BlockSpec((tile, cols), lambda i: (i, 0)),
+            pl.BlockSpec((cols, cols), lambda i: (0, 0), pipeline_mode=pl.Buffered(1)),
+            pl.BlockSpec((tile, cols), lambda i: (i, 0)),
+        ],
+        out_specs=[
+            pl.BlockSpec((tile, cols), lambda i: (i, 0)),
+            pl.BlockSpec((tile, cols), lambda i: (i, 0)),
+        ],
+        scratch_shapes=[pltpu.VMEM((tile, cols), bf16)],
+        compiler_params=pltpu.CompilerParams(vmem_limit_bytes=60 * 2**20),
+        name="newton_schulz",
+    )(x, gram, mom_new)
+    return momentum_out[None], update[None]
+
+
 def solution(mesh):
+    fits = mesh.shape["dp"] == 4 and mesh.shape["group"] == 8
     return jax.shard_map(
-        shards,
+        kernels if fits else shards,
         mesh=mesh,
         in_specs=(P("dp", None, "group", None), P("dp", "group", None)),
         out_specs=(P("dp", "group", None), P("dp", "group", None)),

time: 378 us -> 201 us (0.53)
  waiting for transfers between devices: 299 us -> 0 us
  Pallas kernels: 0 us -> 200 us
  matrix products: 37.8 us -> 0 us
  blocking collectives: 16.6 us -> 0 us
  between operations: 14.5 us -> 0.64 us
  other arithmetic: 7.75 us -> 0 us
    pallas_call x0 -> x2, Pallas kernels: none -> 200 us  [the longest x1 176 us: kernels(): pl.pallas_call(sum_kernel, out_shape=(jax.ShapeDtypeStruct((rows, cols),...]
    unnamed x4 -> x0, waiting for transfers between devices: 144 us -> none
    reduce_scatter x1 -> x0, waiting for transfers between devices: 87.6 us -> none  [orthogonal(): lax.psum_scatter(lax.dot_general(block, block, (((0,), (0,)), ((), ())),...]
    all_gather x1 -> x0, waiting for transfers between devices: 67.3 us -> none  [orthogonal(): gram_full = lax.all_gather(gram_slab, 'group', axis=0, tiled=True)]
    dot_general x3 -> x0, matrix products: 37.8 us -> none  [the longest x1 13.3 us: orthogonal(): lax.dot_general(block, gram_full, (((1,), (1,)), ((), ())), preferred_ele...]
    psum x1 -> x0, blocking collectives: 16.6 us -> none  [orthogonal(): total = lax.psum(jnp.sum(wide * wide), 'group')]
    reduce_sum x1 -> x0, other arithmetic: 7.75 us -> none  [orthogonal(): total = lax.psum(jnp.sum(wide * wide), 'group')]
  transfers between devices with their start and end apart: 3 -> 0, of which waited for: 3 -> 0; matrix products, arithmetic and copies ran while one was open for 0% -> 0% of each run, Pallas kernels for 0% -> 0%
where the time goes in v1:
time: 201 us
  Pallas kernels  200 us (100%)
    pallas_call x1, Pallas kernels, kernels(): pl.pallas_call(sum_kernel, out_shape=(jax.ShapeDtypeStruct((rows, cols),...  176 us
    pallas_call x1, Pallas kernels, kernels(): pl.pallas_call(finish_kernel, grid=(rows // tile,), out_shape=(jax.ShapeD...  24.3 us

profile of v1, /device:TPU:1, one launch (start us, length us, event | category | flops | bytes accessed | tf_op | source)
XLA Modules:
  0.0 200.7 jit_solution(8662991608435031885)
XLA Ops:
  0.6 175.8 %sum_and_gram.1 = (f32[896,2048]{1,0:T(8,128)}, bf16[896,2048]{1,0:T(8,128)(2,1)}, bf16[2048,2048]{1,0:T(8,128)(2,1)}) custom-call(bf16[1,4,896,2048]{3,2,1,0:T(8,128)(2,1)} %partials.1, f32[1,896,2048]{2,1,0:T(8,128)} %momentum.1), custom_call_target="tpu_custom_call" | custom-call | tf_op jit(solution)/shard_map/sum_and_gram/pallas_call | solution.py:429
  176.4 24.3 %newton_schulz.1 = (f32[896,2048]{1,0:T(8,128)}, bf16[896,2048]{1,0:T(8,128)(2,1)}) custom-call(bf16[896,2048]{1,0:T(8,128)(2,1)} %get-tuple-element.7.x_ref, bf16[2048,2048]{1,0:T(8,128)(2,1)} %get-tuple-element.8.gram_ref, f32[896,2048]{1,0:T(8,128)} %get-tuple-element.9.mom_ref), custom_call_target="tpu_custom_call" | custom-call | tf_op jit(solution)/shard_map/newton_schulz/pallas_call | solution.py:471

commit v2 on v1

--- a/solution.py
+++ b/solution.py
@@ -9,7 +9,8 @@
 from jax.sharding import PartitionSpec as P
 
 C = 7168
-NB = 8
+EDGES = (0, 2, 4, 6, 8, 10, 12, 14, 15, 16)
+NB = len(EDGES) - 1
 WINDOW = 2
 MESH = pl.DeviceIdType.MESH
 
@@ -52,6 +53,27 @@
     blended = (grad + 0.95 * momentum_out).astype(jnp.bfloat16)
     results = [orthogonal(blended[0])]
     return (momentum_out, jnp.stack(results))
+
+
+def times_gram(left, gram, edge, k, low, high):
+    at, split = slice(edge[k], edge[k + 1]), edge[k + 1]
+    acc = None
+    if low < split:
+        acc = jnp.dot(
+            left[:, low : min(split, high)],
+            gram[low : min(split, high), at],
+            preferred_element_type=jnp.float32,
+        )
+    if split < high:
+        start = max(split, low)
+        more = lax.dot_general(
+            left[:, start:high],
+            gram[at, start:high],
+            (((1,), (1,)), ((), ())),
+            preferred_element_type=jnp.float32,
+        )
+        acc = more if acc is None else acc + more
+    return acc
 
 
 def sum_kernel(
@@ -87,7 +109,8 @@
     store_sem,
 ):
     rows, cols = x.shape
-    blk = cols // NB
+    wide = cols // 8
+    edge = [e * cols // 16 for e in EDGES]
     half = rows // 2
     dp = lax.axis_index("dp")
     group = lax.axis_index("group")
@@ -113,7 +136,7 @@
     hop2 = [at_y, at_x]
 
     def col(k):
-        return slice(k * blk, (k + 1) * blk)
+        return slice(edge[k], edge[k + 1])
 
     def dp_copy(kind, p, k):
         src, dst, to = (
@@ -152,7 +175,7 @@
         return copies
 
     def stores(k):
-        top = (k + 1) * blk
+        top = edge[k + 1]
         return [
             pltpu.make_async_copy(mom.at[:, col(k)], mom_hbm.at[:, col(k)], store_sem.at[0, k]),
             pltpu.make_async_copy(x.at[:, col(k)], x_hbm.at[:, col(k)], store_sem.at[1, k]),
@@ -177,13 +200,14 @@
             dp_copy(2, p, k).start()
 
     def unit(k):
-        return (k + 1) * blk // 4
+        return edge[k + 1] // 4
 
     def packed(k, h=None):
-        start = blk // 4 * k * (k + 1)
+        start = sum(2 * unit(i) for i in range(k))
+        across = slice(0, edge[k + 1] - edge[k])
         if h is None:
-            return slice(start, start + 2 * unit(k))
-        return slice(start + h * unit(k), start + (h + 1) * unit(k))
+            return slice(start, start + 2 * unit(k)), across
+        return slice(start + h * unit(k), start + (h + 1) * unit(k)), across
 
     def pair_copy(k):
         return pltpu.make_async_remote_copy(
@@ -214,13 +238,22 @@
             copy.start()
         own = x[at]
 
-        @pl.loop(0, k + 1)
+        width = edge[k + 1] - edge[k]
+
+        def strip(at):
+            part[at, :width] = jnp.dot(xt[at, :], own, preferred_element_type=jnp.float32)
+
+        whole = edge[k + 1] // wide
+
+        @pl.loop(0, whole)
         def _(r):
-            strip = pl.ds(pl.multiple_of(r * blk, blk), blk)
-            part[strip, :] = jnp.dot(xt[strip, :], own, preferred_element_type=jnp.float32)
+            strip(pl.ds(pl.multiple_of(r * wide, wide), wide))
+
+        if whole * wide < edge[k + 1]:
+            strip(slice(whole * wide, edge[k + 1]))
 
         n = 2 * unit(k)
-        pair_out[packed(k), :] = part[pl.ds(pl.multiple_of(other * n, n), n), :].astype(
+        pair_out[packed(k)] = part[pl.ds(pl.multiple_of(other * n, n), n), :width].astype(
             jnp.bfloat16
         )
         pair_copy(k).start()
@@ -237,7 +270,7 @@
     def red_copy(k, h, to_spot, slot):
         return pltpu.make_async_remote_copy(
             src_ref=sums.at[packed(k, h)],
-            dst_ref=chain.at[slot, packed(k, h)],
+            dst_ref=chain.at[(slot, *packed(k, h))],
             send_sem=red_send.at[h, k],
             recv_sem=red_recv.at[slot, h, k],
             device_id=(dp, chip_at(h, to_spot) * 2 + core),
@@ -267,9 +300,9 @@
     def pair_sum(k):
         pair_copy(k).wait_recv()
         n = 2 * unit(k)
-        sums[packed(k), :] = (
-            part[pl.ds(pl.multiple_of(core * n, n), n), :]
-            + pair_in[packed(k), :].astype(jnp.float32)
+        sums[packed(k)] = (
+            part[pl.ds(pl.multiple_of(core * n, n), n), : edge[k + 1] - edge[k]]
+            + pair_in[packed(k)].astype(jnp.float32)
         ).astype(jnp.bfloat16)
         for h in range(2):
 
@@ -288,8 +321,8 @@
             def _():
                 at = packed(k, h)
                 red_copy(k, h, 2, 0).wait_recv()
-                sums[at, :] = (
-                    sums[at, :].astype(jnp.float32) + chain[0, at, :].astype(jnp.float32)
+                sums[at] = (
+                    sums[at].astype(jnp.float32) + chain[(0, *at)].astype(jnp.float32)
                 ).astype(jnp.bfloat16)
                 red_copy(k, h, 1, 1).start()
 
@@ -302,9 +335,9 @@
                 red_copy(k, h, 1, 0).wait_recv()
                 red_copy(k, h, 1, 1).wait_recv()
                 final(k, h, core)[...] = (
-                    sums[at, :].astype(jnp.float32)
-                    + chain[0, at, :].astype(jnp.float32)
-                    + chain[1, at, :].astype(jnp.float32)
+                    sums[at].astype(jnp.float32)
+                    + chain[(0, *at)].astype(jnp.float32)
+                    + chain[(1, *at)].astype(jnp.float32)
                 ).astype(jnp.bfloat16)
                 bc_copy(k, h, 2, 1).start()
                 bc_copy(k, h, 0, 0).start()
@@ -341,18 +374,32 @@
     stages = (
         (0, forward),
         (0, lambda k: send_first(k + WINDOW) if k + WINDOW < NB else None),
-        (4, spread),
-        (5, leaf),
+        (3, pair_sum),
+        (4, root),
         (6, finish),
         (2, blend),
         (3, relay),
-        (2, pair_sum),
-        (3, root),
+        (4, spread),
+        (5, leaf),
     )
-    for step in range(NB + 6):
+    for step in range(NB + 2):
         for lag, stage in stages:
             if 0 <= step - lag < NB:
                 stage(step - lag)
+    end = NB - 1
+    pair_sum(end)
+    root(end - 1)
+    spread(end - 1)
+    leaf(end - 2)
+    finish(end - 3)
+    finish(end - 2)
+    relay(end)
+    root(end)
+    spread(end)
+    leaf(end - 1)
+    leaf(end)
+    finish(end - 1)
+    finish(end)
 
     for k in range(NB):
         for copy in stores(k):
@@ -379,39 +426,26 @@
 
 def finish_kernel(x_ref, gram_ref, mom_ref, mom_out, update, first):
     cols = x_ref.shape[1]
-    blk = cols // NB
+    edge = [e * cols // 16 for e in EDGES]
     mom_out[...] = mom_ref[...]
-    eye = lax.broadcasted_iota(jnp.int32, (blk, blk), 0) == lax.broadcasted_iota(
-        jnp.int32, (blk, blk), 1
-    )
-    trace = jnp.zeros((blk, blk), jnp.float32)
+    trace = jnp.zeros((1, 1), jnp.float32)
     for k in range(NB):
-        at = slice(k * blk, (k + 1) * blk)
-        trace += jnp.where(eye, gram_ref[at, at].astype(jnp.float32), 0.0)
-    total = jnp.sum(trace) + 1e-06
-    scale2 = jnp.full((1, blk), 2.0 / cols, jnp.float32) * total
+        at, w = slice(edge[k], edge[k + 1]), edge[k + 1] - edge[k]
+        eye = lax.broadcasted_iota(jnp.int32, (w, w), 0) == lax.broadcasted_iota(
+            jnp.int32, (w, w), 1
+        )
+        corner = jnp.where(eye, gram_ref[at, at].astype(jnp.float32), 0.0)
+        trace += jnp.sum(jnp.sum(corner, axis=0, keepdims=True), axis=1, keepdims=True)
+    scale2 = (trace + 1e-06) * (2.0 / cols)
     inv = 1.0 / scale2
     last = lax.rsqrt(scale2) * math.sqrt(C)
 
-    def times_gram(left, k):
-        at, split = slice(k * blk, (k + 1) * blk), (k + 1) * blk
-        acc = jnp.dot(
-            left[:, :split], gram_ref[:split, at], preferred_element_type=jnp.float32
-        )
-        if split < cols:
-            acc += lax.dot_general(
-                left[:, split:],
-                gram_ref[at, split:],
-                (((1,), (1,)), ((), ())),
-                preferred_element_type=jnp.float32,
-            )
-        return acc
-
     for k in range(NB):
-        first[:, k * blk : (k + 1) * blk] = (times_gram(x_ref, k) * inv).astype(jnp.bfloat16)
+        at = slice(edge[k], edge[k + 1])
+        first[:, at] = (times_gram(x_ref, gram_ref, edge, k, 0, cols) * inv).astype(jnp.bfloat16)
     for k in range(NB):
-        at = slice(k * blk, (k + 1) * blk)
-        second = times_gram(first, k) * inv
+        at = slice(edge[k], edge[k + 1])
+        second = times_gram(first, gram_ref, edge, k, 0, cols) * inv
         ortho = (
             3.4445 * x_ref[:, at].astype(jnp.float32)
             - 4.775 * first[:, at].astype(jnp.float32)
@@ -422,8 +456,8 @@
 
 def kernels(partials, momentum):
     _, _, rows, cols = partials.shape
-    blk = cols // NB
-    packed_rows = blk // 4 * NB * (NB + 1)
+    blk = cols // 8
+    packed_rows = sum(e * cols // 32 for e in EDGES)
     bf16, f32 = jnp.bfloat16, jnp.float32
     dma = pltpu.SemaphoreType.DMA
     mom_new, x, gram = pl.pallas_call(

time: 201 us -> 202 us (level)
    pallas_call x1, Pallas kernels: 24.3 us -> 27 us  [kernels(): pl.pallas_call(finish_kernel, grid=(rows // tile,), out_shape=(jax.ShapeD...]
where the time goes in v2:
time: 202 us
  Pallas kernels  201 us (100%)
    pallas_call x1, Pallas kernels, kernels(): pl.pallas_call(sum_kernel, out_shape=(jax.ShapeDtypeStruct((rows, cols),...  174 us
    pallas_call x1, Pallas kernels, kernels(): pl.pallas_call(finish_kernel, grid=(rows // tile,), out_shape=(jax.ShapeD...  27 us

profile of v2, /device:TPU:1, one launch (start us, length us, event | category | flops | bytes accessed | tf_op | source)
XLA Modules:
  0.0 201.8 jit_solution(5470188523591641064)
XLA Ops:
  0.6 174.1 %sum_and_gram.1 = (f32[896,2048]{1,0:T(8,128)}, bf16[896,2048]{1,0:T(8,128)(2,1)}, bf16[2048,2048]{1,0:T(8,128)(2,1)}) custom-call(bf16[1,4,896,2048]{3,2,1,0:T(8,128)(2,1)} %partials.1, f32[1,896,2048]{2,1,0:T(8,128)} %momentum.1), custom_call_target="tpu_custom_call" | custom-call | tf_op jit(solution)/shard_map/sum_and_gram/pallas_call | solution.py:463
  174.8 27.0 %newton_schulz.1 = (f32[896,2048]{1,0:T(8,128)}, bf16[896,2048]{1,0:T(8,128)(2,1)}) custom-call(bf16[896,2048]{1,0:T(8,128)(2,1)} %get-tuple-element.7.x_ref, bf16[2048,2048]{1,0:T(8,128)(2,1)} %get-tuple-element.8.gram_ref, f32[896,2048]{1,0:T(8,128)} %get-tuple-element.9.mom_ref), custom_call_target="tpu_custom_call" | custom-call | tf_op jit(solution)/shard_map/newton_schulz/pallas_call | solution.py:505
